TPU v7x, 32 devices: a whole 2x2x4 slice. The times are simulated.
32 devices in a mesh: rep: 2 (over y), tp: 4 (over z), ad: 4 (over x, core).
Axes of the slice: x: 2, y: 2, z: 4, core: 2. Of those that a mesh axis runs over, the one named last changes fastest.
Arguments:
- tokens: bfloat16 [6144, 8192], P(('rep', 'ad'), 'tp'), parts along dimension 0
- query_base_weight: bfloat16 [8192, 512], P('ad', 'tp'), may hold values from -0.0625 to 0.0625
- adapter_down_weight: bfloat16 [128, 8192, 64], P('ad', 'tp'), may hold values from -0.0625 to 0.0625
- adapter_up_weight: bfloat16 [128, 64, 512], P('ad', None, 'tp'), may hold values from -0.75 to 0.75
- rotated_key_cache: bfloat16 [6144, 4, 128], P(('rep', 'ad')), parts along dimension 0
- value_cache_rows: bfloat16 [6144, 4, 128], P(('rep', 'ad')), parts along dimension 0, may hold values from -6 to 6
- segment_index: int32 [8, 768], P(('rep', 'ad')), parts along dimension 0, may hold values from 0 to 7, never falling along the last dimension, each value on 1 to 256 neighbouring positions
- tenant_index: int32 [8, 8], P(('rep', 'ad')), parts along dimension 0, may hold values from 0 to 127, as said below
Outputs:
- attention: bfloat16 [6144, 512], P(('rep', 'ad'), 'tp'), parts along dimension 0
There are 2 independent parts, one for each index of `rep`. A program takes and returns all parts, laid end to end along the dimension named above; an argument that names none is the same for every part. Nothing has to cross between parts.
Inputs may be any that keep to these rules, and one draw needn't show every extreme that they name: `tenant_index`: adapter a is held by owner a // 32 along ad, in its slot a mod 32. Among the 8 sequences of one batch at most 4 use adapters of one owner, and one owner is used by exactly 4 sequences of every batch. `segment_index`: within a batch segment numbers never fall; sequence s is the tokens numbered s, each has 1 to 256 tokens and one has exactly 256.
All inputs are finite; a program needn't handle non-finite values.
Results may differ from a plain program's by a relative error of at most 0.012.
The roundings to bfloat16 on the way count: a program that leaves them out, or rounds other values in their place, can miss the bound.
Values may be sent and summed in bfloat16 or wider, within the bound.
A program may use at most 192 MiB of HBM per device.

v0:
```python
import jax
import jax.numpy as jnp
from jax import lax
from jax.sharding import PartitionSpec as P

rope_theta = 500000.0
adapter_scale = 0.5


def positions_of(segment_row):
    length = segment_row.shape[0]
    indices = jnp.arange(length, dtype=jnp.int32)
    starting = jnp.concatenate([jnp.ones((1,), jnp.bool_), segment_row[1:] != segment_row[:-1]])
    earliest = lax.cummax(jnp.where(starting, indices, jnp.zeros_like(indices)), axis=0)
    return (indices - earliest).astype(jnp.float32)


def rotate(matrix, position):
    half_width = matrix.shape[-1] // 2
    exponent = jnp.arange(half_width, dtype=jnp.float32) * (2.0 / matrix.shape[-1])
    frequency = jnp.power(jnp.float32(rope_theta), -exponent)
    angles = position[:, None] * frequency[None, :]
    cosine = jnp.cos(angles)
    sine = jnp.sin(angles)
    leading = matrix[..., :half_width]
    trailing = matrix[..., half_width:]
    return jnp.concatenate(
        [leading * cosine - trailing * sine, trailing * cosine + leading * sine], axis=-1
    )


def attend(query_head, key_head, value_head, segment_row):
    length = segment_row.shape[0]
    indices = jnp.arange(length, dtype=jnp.int32)
    scores = jnp.dot(query_head, key_head.T, preferred_element_type=jnp.float32) * (
        1.0 / jnp.sqrt(jnp.float32(query_head.shape[-1]))
    )
    allowed = (segment_row[:, None] == segment_row[None, :]) & (
        indices[None, :] <= indices[:, None]
    )
    masked = jnp.where(allowed, scores, -jnp.inf)
    highest = jnp.max(masked, axis=1, keepdims=True)
    expanded = jnp.where(allowed, jnp.exp(scores - highest), jnp.float32(0.0))
    totals = jnp.sum(expanded, axis=1, keepdims=True)
    probs = (expanded / totals).astype(jnp.bfloat16)
    return jnp.dot(probs, value_head, preferred_element_type=jnp.float32).astype(jnp.bfloat16)


def body(
    tokens,
    query_base_weight,
    adapter_down_weight,
    adapter_up_weight,
    rotated_key_cache,
    value_cache_rows,
    segment_index,
    tenant_index,
):
    segment_row = segment_index[0]
    token_tenants = tenant_index[0]
    sequences = token_tenants.shape[0]
    row_count = tokens.shape[0]
    adapter_rank_width = adapter_down_weight.shape[2]
    head_width = query_base_weight.shape[1]
    feature_matrix = adapter_down_weight.shape[1]
    onehot = segment_row[:, None] == jnp.arange(sequences, dtype=jnp.int32)[None, :]
    gathered = lax.all_gather(tokens, "tp", axis=1, tiled=True)
    base_output = jnp.dot(
        gathered,
        lax.all_gather(query_base_weight, "ad", axis=0, tiled=True),
        preferred_element_type=jnp.float32,
    )
    portions = (
        lax.all_gather(adapter_down_weight, "ad", axis=0, tiled=True),
        lax.all_gather(adapter_up_weight, "ad", axis=0, tiled=True),
    )
    count = portions[0].shape[0]
    lookup = (token_tenants[:, None] == jnp.arange(count, dtype=jnp.int32)[None, :]).astype(
        jnp.bfloat16
    )
    down_part = jnp.einsum("sn,nxr->sxr", lookup, portions[0], preferred_element_type=jnp.float32)
    up_part = jnp.einsum("sn,nrh->srh", lookup, portions[1], preferred_element_type=jnp.float32)
    selected_down = down_part.astype(jnp.bfloat16)
    up_sel = up_part.astype(jnp.bfloat16)
    selected_down, up_sel = (selected_down, up_sel)
    down_flat = jnp.transpose(selected_down, (1, 0, 2)).reshape(
        feature_matrix, sequences * adapter_rank_width
    )
    partial_all = jnp.dot(tokens, down_flat, preferred_element_type=jnp.float32).reshape(
        row_count, sequences, adapter_rank_width
    )
    partial_sum = jnp.sum(jnp.where(onehot[:, :, None], partial_all, jnp.float32(0.0)), axis=1)
    shrink_b = lax.psum(partial_sum, "tp").astype(jnp.bfloat16)
    spread = jnp.where(onehot[:, :, None], shrink_b[:, None, :], jnp.zeros((), jnp.bfloat16))
    flat_rows = spread.reshape(row_count, sequences * adapter_rank_width)
    adapted_queries = jnp.dot(
        flat_rows,
        up_sel.reshape(sequences * adapter_rank_width, head_width),
        preferred_element_type=jnp.float32,
    )
    combined_queries = base_output + adapter_scale * adapted_queries
    queries = rotate(combined_queries, positions_of(segment_row)).astype(jnp.bfloat16)
    heads_total = lax.axis_size("tp")
    kv_heads = rotated_key_cache.shape[1]
    kv_index = lax.axis_index("tp") // (heads_total // kv_heads)
    key_head = lax.dynamic_index_in_dim(rotated_key_cache, kv_index, 1, keepdims=False)
    value_head = lax.dynamic_index_in_dim(value_cache_rows, kv_index, 1, keepdims=False)
    return attend(queries, key_head, value_head, segment_row)


def solution(mesh):
    return jax.shard_map(
        body,
        mesh=mesh,
        in_specs=(
            P(("rep", "ad"), "tp"),
            P("ad", "tp"),
            P("ad", "tp", None),
            P("ad", None, "tp"),
            P(("rep", "ad"), None, None),
            P(("rep", "ad"), None, None),
            P(("rep", "ad"), None),
            P(("rep", "ad"), None),
        ),
        out_specs=P(("rep", "ad"), "tp"),
        check_vma=False,
    )
```

profile of v0, /device:TPU:3, one launch (start us, length us, event | category | flops | bytes accessed | tf_op | source)
XLA Modules:
  0.0 522.9 jit_solution(11916409690093097127)
XLA Ops:
  6.5 0.7 all-gather.11.cloned.1.call-update
  7.3 0.0 all-gather.7.cloned.1.call-start
  7.3 0.7 all-gather.7.cloned.1.call-update
  8.0 0.0 all-gather.5.cloned.1.call-start
  8.1 0.7 all-gather.5.cloned.1.call-update
  8.7 0.0 all-gather.9.cloned.1.call-start
  8.8 11.3 %copy.14 = bf16[32,2048,64]{1,0,2:T(8,128)(2,1)} copy(bf16[32,2048,64]{1,2,0:T(8,128)(2,1)} %param.10) | data formatting | bytes 16777216 | tf_op args[2]
  20.2 0.6 copy-done.3
  20.8 0.1 compare_reduce_fusion
  20.9 0.1 add_select_fusion
  21.0 0.3 reduce-window.9
  21.3 0.1 slice.24
  21.4 0.1 slice_reduce_fusion
  21.5 0.8 constant_dynamic-slice_fusion
  22.3 0.1 fusion.29
  22.4 9.6 %all-gather.11.cloned.1.call-done = bf16[128,64,128]{2,1,0:T(8,128)(2,1)} async-done(((bf16[32,64,128]{2,1,0:T(8,128)(2,1)}), bf16[128,64,128]{2,1,0:T(8,128)(2,1)}) %all-gather.11.cloned.1.call-update) | async-done | bytes 2097168 | tf_op jit(solution)/shard_map/all_gather | solution.py:75
  32.0 2.8 fusion.9
  34.8 21.4 %all-gather.7.cloned.1.call-done = bf16[8192,128]{1,0:T(8,128)(2,1)} async-done(((bf16[2048,128]{1,0:T(8,128)(2,1)}), bf16[8192,128]{1,0:T(8,128)(2,1)}) %all-gather.7.cloned.1.call-update) | async-done | bytes 2097168 | tf_op jit(solution)/shard_map/all_gather | solution.py:70
  56.2 220.8 %all-gather.5.cloned.1.call-done = bf16[768,8192]{1,0:T(8,128)(2,1)} async-done(((bf16[768,2048]{1,0:T(8,128)(2,1)}), bf16[768,8192]{1,0:T(8,128)(2,1)}) %all-gather.5.cloned.1.call-update) | async-done | bytes 12582928 | tf_op jit(solution)/shard_map/all_gather | solution.py:67
  277.0 9.5 %fusion.39 = f32[768,128]{0,1:T(8,128)S(1)} fusion(bf16[768,8192]{1,0:T(8,128)(2,1)} %all-gather.5.cloned.1.call-done, bf16[8192,128]{1,0:T(8,128)(2,1)} %all-gather.7.cloned.1.call-done), kind=kOutput, calls=%fused_computation.56 | convolution fusion | flops 1610612736 | bytes 15073280 | tf_op jit(solution)/shard_map/dot_general | solution.py:68
  286.5 190.8 %all-gather.9.cloned.1.call-done = bf16[128,2048,64]{1,0,2:T(8,128)(2,1)} async-done(((bf16[32,2048,64]{1,0,2:T(8,128)(2,1)}), bf16[128,2048,64]{1,0,2:T(8,128)(2,1)}) %all-gather.9.cloned.1.call-update) | async-done | bytes 33554448 | tf_op jit(solution)/shard_map/all_gather | solution.py:74
  477.2 12.9 %fusion = bf16[2048,8,64]{0,1,2:T(8,128)(2,1)S(1)} fusion(bf16[128,2048,64]{1,0,2:T(8,128)(2,1)} %all-gather.9.cloned.1.call-done, s32[8]{0:T(128)S(1)} %bitcast.41), kind=kOutput, calls=%fused_computation.1 | convolution fusion | flops 269485056 | bytes 35651616 | tf_op jit(solution)/shard_map/sn,nxr->sxr/dot_general | solution.py:81
  490.1 1.2 copy.15
  491.3 0.7 copy-done
  492.0 1.8 fusion.40
  493.8 0.1 select_reduce_fusion.1
  494.0 18.7 %all-reduce.1 = bf16[768,64]{0,1:T(8,128)(2,1)S(1)} all-reduce(f32[768,64]{0,1:T(8,128)S(1)} %select_reduce_fusion.1), channel_id=1, replica_groups=mesh['rep'=2,'tp'=4,'ad'=4] {'tp'}, use_global_device_ids=true, to_apply=%region_1.2 | all-reduce | flops 49152 | bytes 294912 | tf_op jit(solution)/shard_map/psum | solution.py:93
  512.7 0.3 fusion.6
  513.0 0.8 fusion.21
  513.8 0.5 select_reduce_fusion
  514.3 0.5 fusion.4
  514.8 1.5 fusion.8
  (14 shorter events, 0.1 us)
Async XLA Ops:
  6.5 25.5 %all-gather.11.cloned.1.call-start = ((), (), s32[]{:S(2)}) async-start(), calls=%async_computation.3 | async-start | bytes 2621440 | tf_op jit(solution)/shard_map/all_gather | solution.py:75
  7.3 48.9 %all-gather.7.cloned.1.call-start = ((), (), s32[]{:S(2)}) async-start(), calls=%async_computation.1 | async-start | bytes 2621440 | tf_op jit(solution)/shard_map/all_gather | solution.py:70
  8.0 269.0 %all-gather.5.cloned.1.call-start = ((), (), s32[]{:S(2)}) async-start(), calls=%async_computation | async-start | bytes 15728640 | tf_op jit(solution)/shard_map/all_gather | solution.py:67
  8.7 468.5 %all-gather.9.cloned.1.call-start = ((), (), s32[]{:S(2)}) async-start(), calls=%async_computation.2 | async-start | bytes 41943040 | tf_op jit(solution)/shard_map/all_gather | solution.py:74
  20.1 0.7 copy-start.3
  20.1 1.4 copy-start.1
  20.1 1.4 copy-start.2
  20.1 11.9 %copy-start.4 = (s32[1,8]{1,0:T(1,128)S(1)}, s32[1,8]{1,0:T(1,128)}, u32[]{:S(2)}) copy-start(s32[1,8]{1,0:T(1,128)} %param.15) | copy-start | bytes 100
  490.1 1.9 copy-start
Sparse Core Ops, SparseCore 0:
  8.9 23.0 all-gather.10
  33.6 22.5 all-gather.6
  57.8 219.1 all-gather.4
  278.4 198.7 all-gather.8
where the time goes:
time: 529 us; the launch traced here: 523 us
  waiting for transfers between devices  445 us (84%)
  matrix products  29.3 us (6%)
  blocking collectives  18.7 us (4%)
  local copies, waits for them, and re-layouts  14.9 us (3%)
  between operations  13.2 us (2%)
    all_gather x1, waiting for transfers between devices, body(): gathered = lax.all_gather(tokens, 'tp', axis=1, tiled=True)  221 us
    all_gather x1, waiting for transfers between devices, body(): lax.all_gather(adapter_down_weight, 'ad', axis=0, tiled=True)  191 us
    all_gather x1, waiting for transfers between devices, body(): lax.all_gather(query_base_weight, 'ad', axis=0, tiled=True)  21.4 us
    psum x1, blocking collectives, body(): shrink_b = lax.psum(partial_sum, 'tp').astype(jnp.bfloat16)  18.7 us
    dot_general x1, matrix products, body(): jnp.einsum('sn,nxr->sxr', lookup, portions[0], preferred_element_type=jnp...  12.9 us
    unnamed x11, local copies, waits for them, and re-layouts  12.7 us
  transfers between devices with their start and end apart: 4, of which 4 were waited for; matrix products, arithmetic and copies ran while one was open for 5% of the time, Pallas kernels for 0%

commit v1 on v0

--- a/solution.py
+++ b/solution.py
@@ -1,10 +1,17 @@
+import math
+
 import jax
 import jax.numpy as jnp
+import numpy as np
 from jax import lax
+from jax.experimental import pallas as pl
+from jax.experimental.pallas import tpu as pltpu
 from jax.sharding import PartitionSpec as P
 
 rope_theta = 500000.0
 adapter_scale = 0.5
+SLOTS = 4
+MESH = pl.DeviceIdType.MESH
 
 
 def positions_of(segment_row):
@@ -108,9 +115,489 @@
     return attend(queries, key_head, value_head, segment_row)
 
 
+def fused_kernel(
+    tok_hbm,
+    w_hbm,
+    down_hbm,
+    up_ref,
+    key_ref,
+    value_ref,
+    seg_ref,
+    tenant_ref,
+    freq_ref,
+    out_ref,
+    tok,
+    down,
+    weight,
+    send_a,
+    recv_a,
+    send_u,
+    recv_u,
+    tenants,
+    tenant_smem,
+    part_send,
+    part_recv,
+    slot_col,
+    cosine,
+    sine,
+    shrink,
+    packed,
+    quarter_recv,
+    rounded,
+    local_sem,
+    ten_send,
+    ten_recv,
+    ws1,
+    ws2,
+    w_recv,
+    a_send,
+    a_recv,
+    u_send,
+    u_recv,
+    p_send,
+    p_recv,
+    q_send,
+    q_recv,
+    g_send,
+    g_recv,
+):
+    rep, tp, ad = lax.axis_index("rep"), lax.axis_index("tp"), lax.axis_index("ad")
+    rows, depth = tok.shape
+    rank = down.shape[1]
+    held_count = down.shape[0]
+    head = weight.shape[2]
+    sequences = SLOTS * 2
+    core = lax.rem(ad, 2)
+    mate = ad + 1 - 2 * core
+    far0 = lax.rem(ad + 2, 4)
+    far1 = far0 + 1 - 2 * lax.rem(far0, 2)
+    other_rep = 1 - rep
+    lane = lax.broadcasted_iota(jnp.int32, (rows, 128), 1)
+    lane_half = lane // rank
+
+    def remote(src, dst, ss, rs, r=None, t=None, a=None):
+        return pltpu.make_async_remote_copy(
+            src_ref=src,
+            dst_ref=dst,
+            send_sem=ss,
+            recv_sem=rs,
+            device_id=(rep if r is None else r, tp if t is None else t, ad if a is None else a),
+            device_id_type=MESH,
+        )
+
+    load_down = pltpu.make_async_copy(down_hbm, down, local_sem.at[0])
+    load_tok = pltpu.make_async_copy(tok_hbm, tok, local_sem.at[1])
+    load_down.start()
+    load_tok.start()
+
+    barrier = pltpu.get_barrier_semaphore()
+    for dt in range(4):
+        for da in range(4):
+            if dt or da:
+                pl.semaphore_signal(
+                    barrier,
+                    inc=1,
+                    device_id=(rep, lax.rem(tp + dt, 4), lax.rem(ad + da, 4)),
+                    device_id_type=MESH,
+                )
+    pl.semaphore_signal(barrier, inc=1, device_id=(other_rep, tp, ad), device_id_type=MESH)
+    pl.semaphore_wait(barrier, 16)
+
+    tenants[ad] = tenant_ref[...]
+    for d in range(1, 4):
+        peer = lax.rem(ad + d, 4)
+        remote(tenant_ref, tenants.at[ad], ten_send.at[peer], ten_recv.at[ad], a=peer).start()
+
+    part = depth // 4
+
+    def quarter(q):
+        return pl.ds(pl.multiple_of(q * part, part), part)
+
+    for target in range(4):
+        rows_q = quarter(rep * 2 + target % 2)
+        q = rep * 2 + target % 2
+        mine = jnp.logical_and(tp == ad, ad == target)
+
+        @pl.when(mine)
+        def _():
+            pltpu.make_async_copy(
+                w_hbm.at[rows_q], weight.at[tp, rows_q], w_recv.at[tp, q]
+            ).start()
+
+        @pl.when(jnp.logical_not(mine))
+        def _():
+            remote(
+                w_hbm.at[rows_q],
+                weight.at[tp, rows_q],
+                ws1.at[target],
+                w_recv.at[tp, q],
+                t=ad,
+                a=target,
+            ).start()
+
+    seg_row = seg_ref[...]
+    seg_col = jnp.transpose(
+        jnp.broadcast_to(seg_row.astype(jnp.float32), (128, rows)), (1, 0)
+    ).astype(jnp.int32)
+
+    for d in range(1, 4):
+        peer = lax.rem(ad + d, 4)
+        remote(tenant_ref, tenants.at[peer], ten_send.at[peer], ten_recv.at[peer], a=peer).wait()
+    to_smem = pltpu.make_async_copy(tenants, tenant_smem, local_sem.at[2])
+    to_smem.start()
+    to_smem.wait()
+    load_down.wait()
+
+    def picks(batch):
+        chosen = [jnp.int32(0)] * SLOTS
+        count = jnp.int32(0)
+        for s in range(sequences):
+            number = tenant_smem[batch, 0, s]
+            here = number // held_count == ad
+            for c in range(SLOTS):
+                chosen[c] = jnp.where(
+                    jnp.logical_and(here, count == c), lax.rem(number, held_count), chosen[c]
+                )
+            count = count + here.astype(jnp.int32)
+        return chosen
+
+    def fill(target_a, target_u, chosen, pair):
+        for c in (2 * pair, 2 * pair + 1):
+            target_a[pl.ds(c * rank, rank), :] = down[chosen[c]]
+            target_u[pl.ds(c * rank, rank), :] = up_ref[chosen[c]]
+
+    def half(ref, owner, pair):
+        return ref.at[owner, pl.ds(pair * 2 * rank, 2 * rank)]
+
+    picked = {}
+    for pair in range(2):
+        for name, peer in (("far0", far0), ("far1", far1)):
+            if pair == 0:
+                picked[name] = picks(peer)
+            fill(send_a.at[peer], send_u.at[peer], picked[name], pair)
+            remote(
+                half(send_a, peer, pair),
+                half(recv_a, ad, pair),
+                a_send.at[peer, pair],
+                a_recv.at[ad, pair],
+                a=peer,
+            ).start()
+    picked["mate"] = picks(mate)
+    for pair in range(2):
+        fill(send_a.at[mate], send_u.at[mate], picked["mate"], pair)
+        remote(
+            half(send_a, mate, pair),
+            half(recv_a, ad, pair),
+            a_send.at[mate, pair],
+            a_recv.at[ad, pair],
+            a=mate,
+        ).start()
+    for peer in (far0, far1, mate):
+        remote(
+            send_u.at[peer], recv_u.at[ad], u_send.at[peer], u_recv.at[ad], a=peer
+        ).start()
+
+    q_own, q_mate = rep * 2 + core, rep * 2 + 1 - core
+    y_own, y_mate = other_rep * 2 + core, other_rep * 2 + 1 - core
+
+    def w_wait(t, q):
+        remote(
+            weight.at[t, quarter(q)], weight.at[t, quarter(q)], ws1.at[0], w_recv.at[t, q], a=mate
+        ).wait_recv()
+
+    def forward(t, q, k, to_rep):
+        block = weight.at[t, quarter(q)]
+        if to_rep:
+            return remote(block, block, ws2.at[t, k], w_recv.at[t, q], r=other_rep)
+        return remote(block, block, ws2.at[t, k], w_recv.at[t, q], a=mate)
+
+    for d in range(4):
+        t = lax.rem(tp + d, 4)
+        w_wait(t, q_own)
+        forward(t, q_own, 0, True).start()
+        forward(t, q_own, 1, False).start()
+
+    picked["own"] = picks(ad)
+    for pair in range(2):
+        fill(recv_a.at[ad], recv_u.at[ad], picked["own"], pair)
+
+    starts = jnp.zeros((rows, 128), jnp.int32)
+    slots = jnp.zeros((rows, 128), jnp.int32)
+    for s in range(sequences):
+        number = tenant_smem[ad, 0, s]
+        owner = number // held_count
+        before = jnp.int32(0)
+        for e in range(s):
+            before = before + (tenant_smem[ad, 0, e] // held_count == owner).astype(jnp.int32)
+        first = jnp.sum((seg_row < s).astype(jnp.float32), axis=1, keepdims=True)
+        hit = seg_col == s
+        slots = jnp.where(hit, owner * SLOTS + before, slots)
+        starts = jnp.where(hit, first.astype(jnp.int32), starts)
+    slot_col[...] = slots
+    position = (lax.broadcasted_iota(jnp.int32, (rows, 128), 0) - starts).astype(jnp.float32)
+    angles = position * freq_ref[...]
+    cosine[...] = jnp.cos(angles)
+    sine[...] = jnp.where(lane_half == 0, -jnp.sin(angles), jnp.sin(angles))
+    load_tok.wait()
+    shrink[...] = jnp.zeros_like(shrink)
+
+    for d in range(4):
+        t = lax.rem(tp + d, 4)
+        w_wait(t, y_own)
+        forward(t, y_own, 2, False).start()
+
+    tile = 256
+    NT = (((1,), (1,)), ((), ()))
+
+    def base_product(t, target):
+        @pl.loop(0, rows // tile)
+        def _(m):
+            at = pl.ds(pl.multiple_of(m * tile, tile), tile)
+            target[at, :] = jnp.dot(tok[at, :], weight[t], preferred_element_type=jnp.float32)
+
+    for d in (1, 2, 3, 0):
+        t = lax.rem(tp + d, 4)
+        w_wait(t, q_mate)
+        w_wait(t, y_mate)
+        if d:
+            base_product(t, part_send.at[t])
+            remote(part_send.at[t], part_recv.at[tp], p_send.at[t], p_recv.at[tp], t=t).start()
+        else:
+            base_product(t, part_recv.at[tp])
+
+    def shrink_product(owner, pair):
+        @pl.loop(0, rows // tile)
+        def _(m):
+            at = pl.ds(pl.multiple_of(m * tile, tile), tile)
+            product = lax.dot_general(
+                tok[at, :],
+                recv_a[owner, pl.ds(pair * 2 * rank, 2 * rank), :],
+                NT,
+                preferred_element_type=jnp.float32,
+            )
+            wanted = owner * SLOTS + pair * 2 + lane_half[:tile]
+            shrink[at, :] = jnp.where(slot_col[at, :] == wanted, product, shrink[at, :])
+
+    def a_wait(owner, pair):
+        remote(
+            half(recv_a, owner, pair),
+            half(recv_a, owner, pair),
+            a_send.at[owner, pair],
+            a_recv.at[owner, pair],
+            a=owner,
+        ).wait_recv()
+
+    for pair in range(2):
+        shrink_product(ad, pair)
+    for pair in range(2):
+        a_wait(mate, pair)
+        shrink_product(mate, pair)
+    for pair in range(2):
+        for owner in (far0, far1):
+            a_wait(owner, pair)
+            shrink_product(owner, pair)
+
+    both = shrink[...] + pltpu.roll(shrink[...], rank, 1)
+    low = rows // 2
+    packed[...] = jnp.where(lane_half[:low] == 0, both[:low], both[low:])
+    span = low // 4
+
+    def piece(t):
+        return pl.ds(pl.multiple_of(t * span, span), span)
+
+    for d in range(1, 4):
+        t = lax.rem(tp + d, 4)
+        remote(packed.at[piece(t)], quarter_recv.at[tp], q_send.at[t], q_recv.at[tp], t=t).start()
+    quarter_recv[tp] = packed[piece(tp), :]
+    for d in range(1, 4):
+        t = lax.rem(tp + d, 4)
+        remote(packed.at[piece(t)], quarter_recv.at[t], q_send.at[t], q_recv.at[t], t=t).wait_recv()
+    total = (quarter_recv[0] + quarter_recv[1]) + (quarter_recv[2] + quarter_recv[3])
+    rounded[tp] = total.astype(jnp.bfloat16)
+    for d in range(1, 4):
+        t = lax.rem(tp + d, 4)
+        remote(rounded.at[tp], rounded.at[tp], g_send.at[t], g_recv.at[tp], t=t).start()
+
+    for d in range(1, 4):
+        t = lax.rem(tp + d, 4)
+        remote(part_send.at[t], part_recv.at[t], p_send.at[t], p_recv.at[t], t=t).wait()
+        peer = lax.rem(ad + d, 4)
+        remote(send_u.at[peer], recv_u.at[peer], u_send.at[peer], u_recv.at[peer], a=peer).wait()
+        remote(packed.at[piece(t)], quarter_recv.at[t], q_send.at[t], q_recv.at[t], t=t).wait_send()
+        for pair in range(2):
+            remote(
+                half(send_a, peer, pair),
+                half(recv_a, peer, pair),
+                a_send.at[peer, pair],
+                a_recv.at[peer, pair],
+                a=peer,
+            ).wait_send()
+    for d in range(4):
+        forward(d, q_own, 0, True).wait_send()
+        forward(d, q_own, 1, False).wait_send()
+        forward(d, y_own, 2, False).wait_send()
+    for target in range(4):
+        rows_q = quarter(rep * 2 + target % 2)
+        mine = jnp.logical_and(tp == ad, ad == target)
+
+        @pl.when(jnp.logical_not(mine))
+        def _():
+            remote(
+                w_hbm.at[rows_q],
+                weight.at[tp, rows_q],
+                ws1.at[target],
+                w_recv.at[tp, rep * 2 + target % 2],
+                t=ad,
+                a=target,
+            ).wait_send()
+
+    for d in range(1, 4):
+        t = lax.rem(tp + d, 4)
+        remote(rounded.at[t], rounded.at[t], g_send.at[t], g_recv.at[t], t=t).wait()
+
+    scale = 1.0 / math.sqrt(head)
+    half_low = lane_half[:span]
+    top, bottom = [], []
+    for t in range(4):
+        values = rounded[t].astype(jnp.float32)
+        turned = pltpu.roll(values, rank, 1)
+        top.append(jnp.where(half_low == 0, values, turned))
+        bottom.append(jnp.where(half_low == 0, turned, values))
+    shrink[...] = jnp.concatenate(top + bottom, axis=0)
+
+    for start in range(0, rows, tile):
+        at = pl.ds(start, tile)
+        slots_here = slot_col[at, :]
+        shrink_here = shrink[at, :]
+        adapted = jnp.zeros((tile, head), jnp.float32)
+        for owner in range(4):
+            for pair in range(2):
+                wanted = owner * SLOTS + pair * 2 + lane_half[:tile]
+                spread = jnp.where(slots_here == wanted, shrink_here, 0.0).astype(jnp.bfloat16)
+                adapted = adapted + jnp.dot(
+                    spread,
+                    recv_u[owner, pl.ds(pair * 2 * rank, 2 * rank), :],
+                    preferred_element_type=jnp.float32,
+                )
+        base = (part_recv[0, at, :] + part_recv[1, at, :]) + (
+            part_recv[2, at, :] + part_recv[3, at, :]
+        )
+        combined = base + adapter_scale * adapted
+        queries = (
+            combined * cosine[at, :] + pltpu.roll(combined, head // 2, 1) * sine[at, :]
+        ).astype(jnp.bfloat16)
+        first = max(0, start - tile)
+        width = start + tile - first
+        scores = (
+            lax.dot_general(
+                queries, key_ref[pl.ds(first, width), :], NT, preferred_element_type=jnp.float32
+            )
+            * scale
+        )
+        row_at = start + lax.broadcasted_iota(jnp.int32, (tile, width), 0)
+        col_at = first + lax.broadcasted_iota(jnp.int32, (tile, width), 1)
+        row_seg = jnp.transpose(
+            jnp.broadcast_to(seg_row[:, start : start + tile].astype(jnp.float32), (128, tile)),
+            (1, 0),
+        )[:, :1].astype(jnp.int32)
+        allowed = jnp.logical_and(row_seg == seg_row[:, first : first + width], col_at <= row_at)
+        masked = jnp.where(allowed, scores, -jnp.inf)
+        highest = jnp.max(masked, axis=1, keepdims=True)
+        expanded = jnp.where(allowed, jnp.exp(scores - highest), 0.0)
+        probs = (expanded / jnp.sum(expanded, axis=1, keepdims=True)).astype(jnp.bfloat16)
+        out_ref[at, :] = jnp.dot(
+            probs, value_ref[pl.ds(first, width), :], preferred_element_type=jnp.float32
+        ).astype(jnp.bfloat16)
+
+
+def fused_body(
+    tokens,
+    query_base_weight,
+    adapter_down_weight,
+    adapter_up_weight,
+    rotated_key_cache,
+    value_cache_rows,
+    segment_index,
+    tenant_index,
+):
+    rows, depth = tokens.shape
+    held, _, rank = adapter_down_weight.shape
+    head = query_base_weight.shape[1]
+    kv_index = lax.axis_index("tp") // (lax.axis_size("tp") // rotated_key_cache.shape[1])
+    key_head = lax.dynamic_index_in_dim(rotated_key_cache, kv_index, 1, keepdims=False)
+    value_head = lax.dynamic_index_in_dim(value_cache_rows, kv_index, 1, keepdims=False)
+    tenant_tile = jnp.pad(tenant_index, ((0, 7), (0, 128 - tenant_index.shape[1])))
+    exponent = np.arange(head // 2, dtype=np.float32) * np.float32(2.0 / head)
+    frequency = np.power(np.float32(rope_theta), -exponent).astype(np.float32)
+    freq_row = jnp.asarray(np.concatenate([frequency, frequency])[None, :])
+    bf16, f32 = jnp.bfloat16, jnp.float32
+    DMA = pltpu.SemaphoreType.DMA
+    vmem = pl.BlockSpec(memory_space=pltpu.VMEM)
+    anywhere = pl.BlockSpec(memory_space=pl.ANY)
+    return pl.pallas_call(
+        fused_kernel,
+        out_shape=jax.ShapeDtypeStruct((rows, head), bf16),
+        in_specs=[anywhere] * 3 + [vmem] * 6,
+        out_specs=vmem,
+        scratch_shapes=[
+            pltpu.VMEM((rows, depth), bf16),
+            pltpu.VMEM((held, rank, depth), bf16),
+            pltpu.VMEM((4, depth, head), bf16),
+            pltpu.VMEM((4, SLOTS * rank, depth), bf16),
+            pltpu.VMEM((4, SLOTS * rank, depth), bf16),
+            pltpu.VMEM((4, SLOTS * rank, head), bf16),
+            pltpu.VMEM((4, SLOTS * rank, head), bf16),
+            pltpu.VMEM((4, 8, 128), jnp.int32),
+            pltpu.SMEM((4, 8, 128), jnp.int32),
+            pltpu.VMEM((4, rows, head), f32),
+            pltpu.VMEM((4, rows, head), f32),
+            pltpu.VMEM((rows, 128), jnp.int32),
+            pltpu.VMEM((rows, 128), f32),
+            pltpu.VMEM((rows, 128), f32),
+            pltpu.VMEM((rows, 128), f32),
+            pltpu.VMEM((rows // 2, 128), f32),
+            pltpu.VMEM((4, rows // 8, 128), f32),
+            pltpu.VMEM((4, rows // 8, 128), bf16),
+            DMA((3,)),
+            DMA((4,)),
+            DMA((4,)),
+            DMA((4,)),
+            DMA((4, 3)),
+            DMA((4, 4)),
+            DMA((4, 2)),
+            DMA((4, 2)),
+            DMA((4,)),
+            DMA((4,)),
+            DMA((4,)),
+            DMA((4,)),
+            DMA((4,)),
+            DMA((4,)),
+            DMA((4,)),
+            DMA((4,)),
+        ],
+        compiler_params=pltpu.CompilerParams(
+            collective_id=0, has_side_effects=True, vmem_limit_bytes=56 * 1024 * 1024
+        ),
+        cost_estimate=pl.CostEstimate(
+            flops=2 * rows * depth * 12 * head, bytes_accessed=20 << 20, transcendentals=1 << 20
+        ),
+    )(
+        tokens,
+        query_base_weight,
+        jnp.transpose(adapter_down_weight, (0, 2, 1)),
+        adapter_up_weight,
+        key_head,
+        value_head,
+        segment_index,
+        tenant_tile,
+        freq_row,
+    )
+
+
 def solution(mesh):
+    square = dict(mesh.shape) == {"rep": 2, "tp": 4, "ad": 4}
     return jax.shard_map(
-        body,
+        fused_body if square else body,
         mesh=mesh,
         in_specs=(
             P(("rep", "ad"), "tp"),

time: 529 us -> 94.1 us (0.18); the launches traced: 523 us -> 93.9 us
  waiting for transfers between devices: 445 us -> 0 us
  Pallas kernels: 0 us -> 87.4 us
  matrix products: 29.3 us -> 0 us
  blocking collectives: 18.7 us -> 0 us
  between operations: 13.2 us -> 0.01 us
  local copies, waits for them, and re-layouts: 14.9 us -> 6.45 us
    all_gather x4 -> x0, waiting for transfers between devices: 443 us -> none  [the longest x1 221 us: body(): gathered = lax.all_gather(tokens, 'tp', axis=1, tiled=True)]
    pallas_call x0 -> x1, Pallas kernels: none -> 87.4 us  [fused_body(): pl.pallas_call(fused_kernel, out_shape=jax.ShapeDtypeStruct((rows, head),...]
    dot_general x7 -> x0, matrix products: 29.3 us -> none  [the longest x1 12.9 us: body(): jnp.einsum('sn,nxr->sxr', lookup, portions[0], preferred_element_type=jnp...]
    psum x1 -> x0, blocking collectives: 18.7 us -> none  [body(): shrink_b = lax.psum(partial_sum, 'tp').astype(jnp.bfloat16)]
    unnamed x11 -> x3, local copies, waits for them, and re-layouts: 12.7 us -> 3.02 us
  transfers between devices with their start and end apart: 4 -> 0, of which waited for: 4 -> 0; matrix products, arithmetic and copies ran while one was open for 5% -> 0% of each run, Pallas kernels for 0% -> 0%
where the time goes in v1:
time: 94.1 us; the launch traced here: 93.9 us
  Pallas kernels  87.4 us (93%)
  local copies, waits for them, and re-layouts  6.45 us (7%)
    pallas_call x1, Pallas kernels, fused_body(): pl.pallas_call(fused_kernel, out_shape=jax.ShapeDtypeStruct((rows, head),...  87.4 us
    unnamed x3, local copies, waits for them, and re-layouts  3.02 us
    dynamic_slice x1, local copies, waits for them, and re-layouts, fused_body(): lax.dynamic_index_in_dim(value_cache_rows, kv_index, 1, keepdims=False)  2.18 us

profile of v1, /device:TPU:3, one launch (start us, length us, event | category | flops | bytes accessed | tf_op | source)
XLA Modules:
  0.0 93.9 jit_solution(708568030052544610)
XLA Ops:
  0.0 2.2 %constant_dynamic-slice_fusion = (bf16[768,1,128]{2,1,0:T(2,128)(2,1)S(1)}, bf16[768,1,128]{2,1,0:T(2,128)(2,1)S(1)}) fusion(bf16[768,4,128]{2,1,0:T(4,128)(2,1)} %param.14, s32[]{:T(128)S(6)} %select_n.8, bf16[768,4,128]{2,1,0:T(4,128)(2,1)} %param.13), kind=kLoop, calls=%fused_computation.2 | loop fusion | bytes 786436 | tf_op jit(solution)/shard_map/jit(dynamic_index_in_dim)/dynamic_slice | solution.py:528
  2.2 0.7 copy.16
  2.9 0.7 copy.17
  3.6 1.2 %pad.4.tenant_ref = s32[8,128]{1,0:T(8,128)} pad(s32[1,8]{1,0:T(1,128)} %param.16, s32[]{:T(128)} %constant.23.clone.1), padding=0_7x0_120 | pad | bytes 4132 | tf_op jit(solution)/shard_map/jit(_pad)/pad | solution.py:529
  4.8 87.4 %shard_map.91 = bf16[768,128]{1,0:T(8,128)(2,1)} custom-call(bf16[768,2048]{1,0:T(8,128)(2,1)} %tok_hbm.1, bf16[2048,128]{1,0:T(8,128)(2,1)} %w_hbm.1, bf16[32,64,2048]{2,1,0:T(8,128)(2,1)} %bitcast.9, bf16[32,64,128]{2,1,0:T(8,128)(2,1)} %up_ref.1, bf16[768,128]{1,0:T(8,128)(2,1)} %bitcast.8, bf16[768,128]{1,0:T(8,128)(2,1)} %bitcast.7, s32[1,768]{1,0:T(1,128)} %seg_ref.1, ...), custom_call_target="tpu_custom_call" | custom-call | flops 4831838208 | bytes 20971520 | tf_op jit(solution)/shard_map/pallas_call | solution.py:537
  92.3 1.6 %copy.19 = bf16[768,128]{1,0:T(8,128)(2,1)} copy(bf16[768,128]{1,0:T(8,128)(2,1)} %shard_map.91) | data formatting | bytes 393216

commit v2 on v1

--- a/solution.py
+++ b/solution.py
@@ -125,6 +125,8 @@
     seg_ref,
     tenant_ref,
     freq_ref,
+    cos_ref,
+    sin_ref,
     out_ref,
     tok,
     down,
@@ -137,6 +139,9 @@
     tenant_smem,
     part_send,
     part_recv,
+    part_own,
+    wide_send,
+    wide_recv,
     slot_col,
     cosine,
     sine,
@@ -144,6 +149,8 @@
     packed,
     quarter_recv,
     rounded,
+    key_head,
+    value_head,
     local_sem,
     ten_send,
     ten_recv,
@@ -203,10 +210,11 @@
     pl.semaphore_signal(barrier, inc=1, device_id=(other_rep, tp, ad), device_id_type=MESH)
     pl.semaphore_wait(barrier, 16)
 
-    tenants[ad] = tenant_ref[...]
+    tenants[ad] = jnp.zeros(tenants.shape[1:], jnp.int32)
+    tenants[ad, 0:1, 0 : tenant_ref.shape[1]] = tenant_ref[...]
     for d in range(1, 4):
         peer = lax.rem(ad + d, 4)
-        remote(tenant_ref, tenants.at[ad], ten_send.at[peer], ten_recv.at[ad], a=peer).start()
+        remote(tenants.at[ad], tenants.at[ad], ten_send.at[peer], ten_recv.at[ad], a=peer).start()
 
     part = depth // 4
 
@@ -242,7 +250,7 @@
 
     for d in range(1, 4):
         peer = lax.rem(ad + d, 4)
-        remote(tenant_ref, tenants.at[peer], ten_send.at[peer], ten_recv.at[peer], a=peer).wait()
+        remote(tenants.at[peer], tenants.at[peer], ten_send.at[peer], ten_recv.at[peer], a=peer).wait()
     to_smem = pltpu.make_async_copy(tenants, tenant_smem, local_sem.at[2])
     to_smem.start()
     to_smem.wait()
@@ -321,30 +329,39 @@
     for pair in range(2):
         fill(recv_a.at[ad], recv_u.at[ad], picked["own"], pair)
 
-    starts = jnp.zeros((rows, 128), jnp.int32)
+    for d in range(4):
+        t = lax.rem(tp + d, 4)
+        w_wait(t, y_own)
+        forward(t, y_own, 2, False).start()
+
+    firsts = jnp.sum(
+        (
+            jnp.broadcast_to(seg_row, (sequences, rows))
+            < lax.broadcasted_iota(jnp.int32, (sequences, rows), 0)
+        ).astype(jnp.float32),
+        axis=1,
+        keepdims=True,
+    )
+    first_angles = firsts * freq_ref[...]
+    first_cos, first_sin = jnp.cos(first_angles), jnp.sin(first_angles)
     slots = jnp.zeros((rows, 128), jnp.int32)
+    start_cos = jnp.zeros((rows, 128), jnp.float32)
+    start_sin = jnp.zeros((rows, 128), jnp.float32)
     for s in range(sequences):
-        number = tenant_smem[ad, 0, s]
-        owner = number // held_count
+        owner = tenant_smem[ad, 0, s] // held_count
         before = jnp.int32(0)
         for e in range(s):
             before = before + (tenant_smem[ad, 0, e] // held_count == owner).astype(jnp.int32)
-        first = jnp.sum((seg_row < s).astype(jnp.float32), axis=1, keepdims=True)
         hit = seg_col == s
         slots = jnp.where(hit, owner * SLOTS + before, slots)
-        starts = jnp.where(hit, first.astype(jnp.int32), starts)
+        start_cos = jnp.where(hit, first_cos[s : s + 1], start_cos)
+        start_sin = jnp.where(hit, first_sin[s : s + 1], start_sin)
     slot_col[...] = slots
-    position = (lax.broadcasted_iota(jnp.int32, (rows, 128), 0) - starts).astype(jnp.float32)
-    angles = position * freq_ref[...]
-    cosine[...] = jnp.cos(angles)
-    sine[...] = jnp.where(lane_half == 0, -jnp.sin(angles), jnp.sin(angles))
+    cosine[...] = cos_ref[...] * start_cos + sin_ref[...] * start_sin
+    turn = sin_ref[...] * start_cos - cos_ref[...] * start_sin
+    sine[...] = jnp.where(lane_half == 0, -turn, turn)
+    shrink[...] = jnp.zeros_like(shrink)
     load_tok.wait()
-    shrink[...] = jnp.zeros_like(shrink)
-
-    for d in range(4):
-        t = lax.rem(tp + d, 4)
-        w_wait(t, y_own)
-        forward(t, y_own, 2, False).start()
 
     tile = 256
     NT = (((1,), (1,)), ((), ()))
@@ -353,17 +370,30 @@
         @pl.loop(0, rows // tile)
         def _(m):
             at = pl.ds(pl.multiple_of(m * tile, tile), tile)
-            target[at, :] = jnp.dot(tok[at, :], weight[t], preferred_element_type=jnp.float32)
+            product = jnp.dot(tok[at, :], weight[t], preferred_element_type=jnp.float32)
+            target[at, :] = product.astype(target.dtype)
+
+    def next_to(t):
+        return jnp.logical_and(t < tp + 3, tp < t + 3)
 
     for d in (1, 2, 3, 0):
         t = lax.rem(tp + d, 4)
         w_wait(t, q_mate)
         w_wait(t, y_mate)
         if d:
-            base_product(t, part_send.at[t])
-            remote(part_send.at[t], part_recv.at[tp], p_send.at[t], p_recv.at[tp], t=t).start()
+
+            @pl.when(next_to(t))
+            def _():
+                base_product(t, wide_send.at[t])
+                remote(wide_send.at[t], wide_recv.at[tp], p_send.at[t], p_recv.at[tp], t=t).start()
+
+            @pl.when(jnp.logical_not(next_to(t)))
+            def _():
+                base_product(t, part_send.at[t])
+                remote(part_send.at[t], part_recv.at[tp], p_send.at[t], p_recv.at[tp], t=t).start()
+
         else:
-            base_product(t, part_recv.at[tp])
+            base_product(t, part_own)
 
     def shrink_product(owner, pair):
         @pl.loop(0, rows // tile)
@@ -392,6 +422,16 @@
     for pair in range(2):
         a_wait(mate, pair)
         shrink_product(mate, pair)
+    kv_index = tp // (4 // key_ref.shape[1])
+    for source, chosen in ((key_ref, key_head), (value_ref, value_head)):
+
+        @pl.loop(0, rows // 128)
+        def _(m):
+            at = pl.ds(pl.multiple_of(m * 128, 128), 128)
+            block = source[at].astype(jnp.float32)
+            kept = lax.broadcasted_iota(jnp.int32, block.shape, 1) == kv_index
+            chosen[at, :] = jnp.sum(jnp.where(kept, block, 0.0), axis=1).astype(jnp.bfloat16)
+
     for pair in range(2):
         for owner in (far0, far1):
             a_wait(owner, pair)
@@ -420,7 +460,17 @@
 
     for d in range(1, 4):
         t = lax.rem(tp + d, 4)
-        remote(part_send.at[t], part_recv.at[t], p_send.at[t], p_recv.at[t], t=t).wait()
+
+        @pl.when(next_to(t))
+        def _():
+            remote(wide_send.at[t], wide_recv.at[t], p_send.at[t], p_recv.at[t], t=t).wait()
+            part_own[...] += wide_recv[t]
+
+        @pl.when(jnp.logical_not(next_to(t)))
+        def _():
+            remote(part_send.at[t], part_recv.at[t], p_send.at[t], p_recv.at[t], t=t).wait()
+            part_own[...] += part_recv[t].astype(jnp.float32)
+
         peer = lax.rem(ad + d, 4)
         remote(send_u.at[peer], recv_u.at[peer], u_send.at[peer], u_recv.at[peer], a=peer).wait()
         remote(packed.at[piece(t)], quarter_recv.at[t], q_send.at[t], q_recv.at[t], t=t).wait_send()
@@ -479,10 +529,7 @@
                     recv_u[owner, pl.ds(pair * 2 * rank, 2 * rank), :],
                     preferred_element_type=jnp.float32,
                 )
-        base = (part_recv[0, at, :] + part_recv[1, at, :]) + (
-            part_recv[2, at, :] + part_recv[3, at, :]
-        )
-        combined = base + adapter_scale * adapted
+        combined = part_own[at, :] + adapter_scale * adapted
         queries = (
             combined * cosine[at, :] + pltpu.roll(combined, head // 2, 1) * sine[at, :]
         ).astype(jnp.bfloat16)
@@ -490,7 +537,7 @@
         width = start + tile - first
         scores = (
             lax.dot_general(
-                queries, key_ref[pl.ds(first, width), :], NT, preferred_element_type=jnp.float32
+                queries, key_head[pl.ds(first, width), :], NT, preferred_element_type=jnp.float32
             )
             * scale
         )
@@ -506,7 +553,7 @@
         expanded = jnp.where(allowed, jnp.exp(scores - highest), 0.0)
         probs = (expanded / jnp.sum(expanded, axis=1, keepdims=True)).astype(jnp.bfloat16)
         out_ref[at, :] = jnp.dot(
-            probs, value_ref[pl.ds(first, width), :], preferred_element_type=jnp.float32
+            probs, value_head[pl.ds(first, width), :], preferred_element_type=jnp.float32
         ).astype(jnp.bfloat16)
 
 
@@ -523,13 +570,11 @@
     rows, depth = tokens.shape
     held, _, rank = adapter_down_weight.shape
     head = query_base_weight.shape[1]
-    kv_index = lax.axis_index("tp") // (lax.axis_size("tp") // rotated_key_cache.shape[1])
-    key_head = lax.dynamic_index_in_dim(rotated_key_cache, kv_index, 1, keepdims=False)
-    value_head = lax.dynamic_index_in_dim(value_cache_rows, kv_index, 1, keepdims=False)
-    tenant_tile = jnp.pad(tenant_index, ((0, 7), (0, 128 - tenant_index.shape[1])))
     exponent = np.arange(head // 2, dtype=np.float32) * np.float32(2.0 / head)
     frequency = np.power(np.float32(rope_theta), -exponent).astype(np.float32)
     freq_row = jnp.asarray(np.concatenate([frequency, frequency])[None, :])
+    both = np.concatenate([frequency, frequency]).astype(np.float64)
+    table = np.arange(rows, dtype=np.float64)[:, None] * both[None, :]
     bf16, f32 = jnp.bfloat16, jnp.float32
     DMA = pltpu.SemaphoreType.DMA
     vmem = pl.BlockSpec(memory_space=pltpu.VMEM)
@@ -537,7 +582,7 @@
     return pl.pallas_call(
         fused_kernel,
         out_shape=jax.ShapeDtypeStruct((rows, head), bf16),
-        in_specs=[anywhere] * 3 + [vmem] * 6,
+        in_specs=[anywhere] * 3 + [vmem] * 8,
         out_specs=vmem,
         scratch_shapes=[
             pltpu.VMEM((rows, depth), bf16),
@@ -549,6 +594,9 @@
             pltpu.VMEM((4, SLOTS * rank, head), bf16),
             pltpu.VMEM((4, 8, 128), jnp.int32),
             pltpu.SMEM((4, 8, 128), jnp.int32),
+            pltpu.VMEM((4, rows, head), bf16),
+            pltpu.VMEM((4, rows, head), bf16),
+            pltpu.VMEM((rows, head), f32),
             pltpu.VMEM((4, rows, head), f32),
             pltpu.VMEM((4, rows, head), f32),
             pltpu.VMEM((rows, 128), jnp.int32),
@@ -558,6 +606,8 @@
             pltpu.VMEM((rows // 2, 128), f32),
             pltpu.VMEM((4, rows // 8, 128), f32),
             pltpu.VMEM((4, rows // 8, 128), bf16),
+            pltpu.VMEM((rows, head), bf16),
+            pltpu.VMEM((rows, head), bf16),
             DMA((3,)),
             DMA((4,)),
             DMA((4,)),
@@ -586,11 +636,13 @@
         query_base_weight,
         jnp.transpose(adapter_down_weight, (0, 2, 1)),
         adapter_up_weight,
-        key_head,
-        value_head,
+        rotated_key_cache,
+        value_cache_rows,
         segment_index,
-        tenant_tile,
+        tenant_index,
         freq_row,
+        jnp.asarray(np.cos(table).astype(np.float32)),
+        jnp.asarray(np.sin(table).astype(np.float32)),
     )
 
 

time: 94.1 us -> 86.5 us (0.919)
  local copies, waits for them, and re-layouts: 6.45 us -> 1.62 us
  Pallas kernels: 87.4 us -> 84.7 us
    pallas_call x1, Pallas kernels: 87.4 us -> 84.7 us  [fused_body(): pl.pallas_call(fused_kernel, out_shape=jax.ShapeDtypeStruct((rows, head),...]
    dynamic_slice x1 -> x0, local copies, waits for them, and re-layouts: 2.18 us -> none  [fused_body(): lax.dynamic_index_in_dim(value_cache_rows, kv_index, 1, keepdims=False)]
    unnamed x3 -> x1, local copies, waits for them, and re-layouts: 3.02 us -> 1.62 us
    pad x1 -> x0, local copies, waits for them, and re-layouts: 1.25 us -> none  [fused_body(): jnp.pad(tenant_index, ((0, 7), (0, 128 - tenant_index.shape[1])))]
where the time goes in v2:
time: 86.5 us; the launch traced here: 86.3 us
  Pallas kernels  84.7 us (98%)
  local copies, waits for them, and re-layouts  1.62 us (2%)
    pallas_call x1, Pallas kernels, fused_body(): pl.pallas_call(fused_kernel, out_shape=jax.ShapeDtypeStruct((rows, head),...  84.7 us

profile of v2, /device:TPU:3, one launch (start us, length us, event | category | flops | bytes accessed | tf_op | source)
XLA Modules:
  0.0 86.3 jit_solution(11029445714020432098)
XLA Ops:
  0.0 84.7 %shard_map.109 = bf16[768,128]{1,0:T(8,128)(2,1)} custom-call(bf16[768,2048]{1,0:T(8,128)(2,1)} %tok_hbm.1, bf16[2048,128]{1,0:T(8,128)(2,1)} %w_hbm.1, bf16[32,64,2048]{2,1,0:T(8,128)(2,1)} %bitcast.1, bf16[32,64,128]{2,1,0:T(8,128)(2,1)} %up_ref.1, bf16[768,4,128]{2,1,0:T(4,128)(2,1)} %key_ref.1, bf16[768,4,128]{2,1,0:T(4,128)(2,1)} %value_ref.1, ...), custom_call_target="tpu_custom_call" | custom-call | flops 4831838208 | bytes 20971520 | tf_op jit(solution)/shard_map/pallas_call | solution.py:582
  84.7 1.6 %copy.13 = bf16[768,128]{1,0:T(8,128)(2,1)} copy(bf16[768,128]{1,0:T(8,128)(2,1)} %shard_map.109) | data formatting | bytes 393216

commit v3 on v2

--- a/solution.py
+++ b/solution.py
@@ -374,7 +374,7 @@
             target[at, :] = product.astype(target.dtype)
 
     def next_to(t):
-        return jnp.logical_and(t < tp + 3, tp < t + 3)
+        return jnp.logical_or(t == tp + 1, t + 1 == tp)
 
     for d in (1, 2, 3, 0):
         t = lax.rem(tp + d, 4)
@@ -395,18 +395,20 @@
         else:
             base_product(t, part_own)
 
-    def shrink_product(owner, pair):
+    def shrink_product(owner):
         @pl.loop(0, rows // tile)
         def _(m):
             at = pl.ds(pl.multiple_of(m * tile, tile), tile)
             product = lax.dot_general(
-                tok[at, :],
-                recv_a[owner, pl.ds(pair * 2 * rank, 2 * rank), :],
-                NT,
-                preferred_element_type=jnp.float32,
+                tok[at, :], recv_a[owner], NT, preferred_element_type=jnp.float32
             )
-            wanted = owner * SLOTS + pair * 2 + lane_half[:tile]
-            shrink[at, :] = jnp.where(slot_col[at, :] == wanted, product, shrink[at, :])
+            kept = shrink[at, :]
+            for pair in range(2):
+                wanted = owner * SLOTS + pair * 2 + lane_half[:tile]
+                kept = jnp.where(
+                    slot_col[at, :] == wanted, product[:, pair * 128 : pair * 128 + 128], kept
+                )
+            shrink[at, :] = kept
 
     def a_wait(owner, pair):
         remote(
@@ -417,11 +419,10 @@
             a=owner,
         ).wait_recv()
 
-    for pair in range(2):
-        shrink_product(ad, pair)
+    shrink_product(ad)
     for pair in range(2):
         a_wait(mate, pair)
-        shrink_product(mate, pair)
+    shrink_product(mate)
     kv_index = tp // (4 // key_ref.shape[1])
     for source, chosen in ((key_ref, key_head), (value_ref, value_head)):
 
@@ -432,10 +433,10 @@
             kept = lax.broadcasted_iota(jnp.int32, block.shape, 1) == kv_index
             chosen[at, :] = jnp.sum(jnp.where(kept, block, 0.0), axis=1).astype(jnp.bfloat16)
 
-    for pair in range(2):
-        for owner in (far0, far1):
+    for owner in (far0, far1):
+        for pair in range(2):
             a_wait(owner, pair)
-            shrink_product(owner, pair)
+        shrink_product(owner)
 
     both = shrink[...] + pltpu.roll(shrink[...], rank, 1)
     low = rows // 2

time: 86.5 us -> 82.5 us (0.954)
  Pallas kernels: 84.7 us -> 79.9 us
    pallas_call x1, Pallas kernels: 84.7 us -> 79.9 us  [fused_body(): pl.pallas_call(fused_kernel, out_shape=jax.ShapeDtypeStruct((rows, head),...]
where the time goes in v3:
time: 82.5 us; the launch traced here: 81.5 us
  Pallas kernels  79.9 us (97%)
  local copies, waits for them, and re-layouts  1.62 us (2%)
    pallas_call x1, Pallas kernels, fused_body(): pl.pallas_call(fused_kernel, out_shape=jax.ShapeDtypeStruct((rows, head),...  79.9 us

profile of v3, /device:TPU:3, one launch (start us, length us, event | category | flops | bytes accessed | tf_op | source)
XLA Modules:
  0.0 81.5 jit_solution(10101796111942220567)
XLA Ops:
  0.0 79.9 %shard_map.109 = bf16[768,128]{1,0:T(8,128)(2,1)} custom-call(bf16[768,2048]{1,0:T(8,128)(2,1)} %tok_hbm.1, bf16[2048,128]{1,0:T(8,128)(2,1)} %w_hbm.1, bf16[32,64,2048]{2,1,0:T(8,128)(2,1)} %bitcast.1, bf16[32,64,128]{2,1,0:T(8,128)(2,1)} %up_ref.1, bf16[768,4,128]{2,1,0:T(4,128)(2,1)} %key_ref.1, bf16[768,4,128]{2,1,0:T(4,128)(2,1)} %value_ref.1, ...), custom_call_target="tpu_custom_call" | custom-call | flops 4831838208 | bytes 20971520 | tf_op jit(solution)/shard_map/pallas_call | solution.py:583
  79.9 1.6 %copy.13 = bf16[768,128]{1,0:T(8,128)(2,1)} copy(bf16[768,128]{1,0:T(8,128)(2,1)} %shard_map.109) | data formatting | bytes 393216
